TPU v7x, 32 devices: a whole 2x2x4 slice. The times are simulated.
32 devices in a mesh: section: 16 (over z, y, core), tensor: 2 (over x).
Axes of the slice: x: 2, y: 2, z: 4, core: 2. Of those that a mesh axis runs over, the one named last changes fastest.
Arguments:
- memory: bfloat16 [2, 12288, 4096], P(None, 'section', 'tensor'), may hold values from -4 to 4
- queries: bfloat16 [4096, 4096], P(('section', 'tensor')), may hold values from -6.5 to 6.5
- out_grad: bfloat16 [4096, 4096], P(('section', 'tensor')), may hold values from -6 to 6
- enc_lengths: int32 [16, 8], replicated, may hold values from 1 to 128, 768 in all within a row
- dec_lengths: int32 [16, 8], replicated, may hold values from 1 to 64, 256 in all within a row
- readers: int32 [16, 8], replicated, may hold values from 0 to 15, as said below
Outputs:
- attended: bfloat16 [4096, 4096], P(('section', 'tensor'))
- query_grad: bfloat16 [4096, 4096], P(('section', 'tensor'))
- memory_grad: bfloat16 [2, 12288, 4096], P(None, 'section', 'tensor')
Inputs may be any that keep to these rules, and one draw needn't show every extreme that they name: `readers`: the reader of example j of encoder device s is (s + k * 2 + 1) modulo 16 for some k < 8; each encoder device names each of its 8 such devices exactly 1 times, so every decoder device is named exactly 8 times.
All inputs are finite; a program needn't handle non-finite values.
Results may differ from a plain program's by a relative error of at most 0.011.
Values may be sent and summed in bfloat16 or wider, within the bound.
A program may use at most 64 MiB of HBM per device.

v0:
```python
import functools

import jax
import jax.numpy as jnp
from jax import lax
from jax.experimental import pallas as pl
from jax.experimental.pallas import tpu as pltpu
from jax.sharding import PartitionSpec as P

HD = 128
ENC_MAX = 128
DEC_MAX = 64
PARTNERS = 8
MOST_CHUNKS = 8
BF16 = jnp.bfloat16
F32 = jnp.float32
MESH = pl.DeviceIdType.MESH


def matmul(a, b, dims):
    return lax.dot_general(a, b, (dims, ((), ())), preferred_element_type=F32)


NN = ((1,), (0,))
NT = ((1,), (1,))
TN = ((0,), (0,))


def chunk_count(width):
    return min(MOST_CHUNKS, width // HD)


def kernel(
    sections,
    tensors,
    mem_hbm,
    q_hbm,
    g_hbm,
    enc_hbm,
    dec_hbm,
    readers_hbm,
    att_out,
    qg_out,
    mg_out,
    mem_v,
    dec_v,
    fsend,
    frecv,
    osend,
    oret,
    fin_v,
    kv_x,
    d_x,
    pack_m,
    unpack_m,
    enc_m,
    grad_m,
    enc_len,
    dec_len,
    readers,
    meta,
    a_send,
    a_recv,
    a_local,
    f_send,
    f_recv,
    o_send,
    o_recv,
    g_send,
    g_recv,
    g_local,
    m_in,
    s_in,
):
    me = lax.axis_index("section")
    mine = lax.axis_index("tensor")
    rows = q_hbm.shape[0]
    enc_count = mem_v.shape[1]
    dec_count = dec_v.shape[2]
    width = mem_v.shape[2]
    chunks = chunk_count(width)
    piece = width // chunks
    spacing = sections // PARTNERS
    scaling = HD ** (-0.5)

    def holder_of(slot):
        return lax.rem(me + 2 * sections - slot * spacing - 1, sections)

    def reader_of(slot):
        return lax.rem(me + slot * spacing + 1, sections)

    half = PARTNERS // 2

    def peer_of(step):
        return lax.rem(mine + step, tensors)

    mem_copy = pltpu.make_async_copy(mem_hbm, mem_v, m_in)
    scalar_copies = [
        pltpu.make_async_copy(source, target, s_in.at[i])
        for i, (source, target) in enumerate(
            ((enc_hbm, enc_len), (dec_hbm, dec_len), (readers_hbm, readers))
        )
    ]
    for copy in scalar_copies:
        copy.start()

    barrier = pltpu.get_barrier_semaphore()
    for step in range(1, tensors):
        pl.semaphore_signal(
            barrier, inc=1, device_id={"tensor": peer_of(step)}, device_id_type=MESH
        )
    for slot in range(PARTNERS):
        pl.semaphore_signal(
            barrier, inc=1, device_id={"section": holder_of(slot)}, device_id_type=MESH
        )
        pl.semaphore_signal(
            barrier, inc=1, device_id={"section": reader_of(slot)}, device_id_type=MESH
        )
    pl.semaphore_wait(barrier, tensors - 1 + 2 * PARTNERS)

    own_rows = pl.ds(pl.multiple_of(mine * rows, rows), rows)

    def first_copy(c, a, step):
        peer = peer_of(step)
        source = (q_hbm, g_hbm)[a]
        columns = pl.ds(pl.multiple_of(peer * width + c * piece, piece), piece)
        if step == 0:
            return pltpu.make_async_copy(
                source.at[:, columns], dec_v.at[c, a, own_rows], a_local.at[c, a]
            )
        return pltpu.make_async_remote_copy(
            src_ref=source.at[:, columns],
            dst_ref=dec_v.at[c, a, own_rows],
            send_sem=a_send.at[c, a, step - 1],
            recv_sem=a_recv.at[c, a, step - 1],
            device_id={"tensor": peer},
            device_id_type=MESH,
        )

    def fetch(c):
        for a in range(2):
            for step in list(range(1, tensors)) + [0]:
                first_copy(c, a, step).start()

    fetch(0)
    mem_copy.start()
    for copy in scalar_copies:
        copy.wait()

    start = jnp.int32(0)
    for i in range(PARTNERS):
        length = dec_len[i, me]
        meta[0, i] = start
        meta[1, i] = length
        start = start + length
    for slot in range(PARTNERS):
        reader = reader_of(slot)
        start, begin, size = jnp.int32(0), jnp.int32(0), jnp.int32(0)
        for j in range(PARTNERS):
            length = enc_len[j, me]
            match = readers[j, me] == reader
            begin = jnp.where(match, start, begin)
            size = jnp.where(match, length, size)
            start = start + length
        meta[2, slot] = begin
        meta[3, slot] = size

    def one_hot(hits):
        return jnp.where(hits, 1.0, 0.0).astype(BF16)

    def iota(shape, dim):
        return lax.broadcasted_iota(jnp.int32, shape, dim)

    for i in range(PARTNERS):
        shape = (DEC_MAX, dec_count)
        within = iota(shape, 0)
        hits = (iota(shape, 1) - within == meta[0, i]) & (within < meta[1, i])
        pack_m[i // half, (i % half) * DEC_MAX : (i % half + 1) * DEC_MAX, :] = one_hot(hits)

    def forward_copy(c, slot):
        holder = holder_of(slot)
        return pltpu.make_async_remote_copy(
            src_ref=fsend.at[c, :, lax.div(holder, spacing)],
            dst_ref=frecv.at[c, :, slot],
            send_sem=f_send.at[c, slot],
            recv_sem=f_recv.at[c, slot],
            device_id={"section": holder},
            device_id_type=MESH,
        )

    def back_copy(c, slot):
        return pltpu.make_async_remote_copy(
            src_ref=osend.at[c, :, slot],
            dst_ref=oret.at[c, :, lax.div(me, spacing)],
            send_sem=o_send.at[c, slot],
            recv_sem=o_recv.at[c, lax.div(me, spacing)],
            device_id={"section": reader_of(slot)},
            device_id_type=MESH,
        )

    def back_arrival(c, i):
        return pltpu.make_async_remote_copy(
            src_ref=osend.at[c, :, i],
            dst_ref=oret.at[c, :, i],
            send_sem=o_send.at[c, i],
            recv_sem=o_recv.at[c, i],
            device_id={"section": reader_of(i)},
            device_id_type=MESH,
        )

    def last_copy(c, a, step):
        peer = peer_of(step)
        target = (att_out, qg_out)[a]
        source = fin_v.at[c, a, pl.ds(pl.multiple_of(peer * rows, rows), rows)]
        columns = pl.ds(pl.multiple_of(mine * width + c * piece, piece), piece)
        if step == 0:
            return pltpu.make_async_copy(source, target.at[:, columns], g_local.at[c, a])
        return pltpu.make_async_remote_copy(
            src_ref=source,
            dst_ref=target.at[:, columns],
            send_sem=g_send.at[c, a, step - 1],
            recv_sem=g_recv.at[c, a, step - 1],
            device_id={"tensor": peer},
            device_id_type=MESH,
        )

    def pack(c):
        for a in range(2):
            first_copy(c, a, 0).wait()
            for step in range(1, tensors):
                first_copy(c, a, step).wait_recv()
        if c + 1 < chunks:
            fetch(c + 1)
        for a in range(2):
            for g in range(2):
                block = matmul(pack_m[g], dec_v[c, a], NN).astype(BF16)
                fsend[c, a, g * half : (g + 1) * half] = block.reshape(half, DEC_MAX, piece)

        @pl.loop(0, PARTNERS)
        def _(turn):
            forward_copy(c, turn).start()

    def expand(c):
        @pl.loop(0, PARTNERS // 2)
        def _(g):
            for a in range(2):
                block = matmul(enc_m[g], mem_v[a, :, c * piece : (c + 1) * piece], NN)
                kv_x[c, a, pl.ds(g * 2, 2)] = block.astype(BF16).reshape(2, ENC_MAX, piece)

    def attend(c):
        @pl.loop(0, PARTNERS)
        def _(turn):
            slot = turn
            forward_copy(c, slot).wait_recv()
            valid = iota((DEC_MAX, ENC_MAX), 1) < meta[3, slot]
            for h in range(piece // HD):
                at = slice(h * HD, (h + 1) * HD)
                q = frecv[c, 0, slot, :, at]
                g = frecv[c, 1, slot, :, at]
                k = kv_x[c, 0, slot, :, at]
                v = kv_x[c, 1, slot, :, at]
                scores = jnp.where(valid, matmul(q, k, NT) * scaling, -jnp.inf)
                weights = jnp.exp(scores - jnp.max(scores, axis=1, keepdims=True))
                probs = weights / jnp.sum(weights, axis=1, keepdims=True)
                low = probs.astype(BF16)
                dprobs = matmul(g, v, NT)
                delta = jnp.sum(probs * dprobs, axis=1, keepdims=True)
                dscores = (probs * (dprobs - delta)).astype(BF16)
                osend[c, 0, slot, :, at] = matmul(low, v, NN).astype(BF16)
                osend[c, 1, slot, :, at] = (matmul(dscores, k, NN) * scaling).astype(BF16)
                d_x[0, slot, :, at] = (matmul(dscores, q, TN) * scaling).astype(BF16)
                d_x[1, slot, :, at] = matmul(low, g, TN).astype(BF16)
            back_copy(c, slot).start()

    def collect(c):
        @pl.loop(0, enc_count // 256)
        def _(b):
            at = pl.ds(pl.multiple_of(b * 256, 256), 256)
            for a in range(2):
                block = d_x[a].reshape(PARTNERS * ENC_MAX, piece)
                mg_out[a, at, c * piece : (c + 1) * piece] = matmul(
                    grad_m[at, :], block, NN
                ).astype(BF16)

    def finish(c):
        @pl.loop(0, PARTNERS)
        def _(i):
            back_arrival(c, i).wait_recv()

        for a in range(2):
            block = oret[c, a].reshape(PARTNERS * DEC_MAX, piece)
            fin_v[c, a] = matmul(unpack_m[...], block, NN).astype(BF16)
            for step in list(range(1, tensors)) + [0]:
                last_copy(c, a, step).start()

    def settle():
        for c in range(chunks):
            for a in range(2):
                for step in range(1, tensors):
                    first_copy(c, a, step).wait_send()

            @pl.loop(0, PARTNERS)
            def _(slot):
                forward_copy(c, slot).wait_send()
                back_copy(c, slot).wait_send()

    pack(0)

    for slot in range(PARTNERS):
        shape = (ENC_MAX, enc_count)
        within = iota(shape, 0)
        hits = (iota(shape, 1) - within == meta[2, slot]) & (within < meta[3, slot])
        enc_m[slot // 2, (slot % 2) * ENC_MAX : (slot % 2 + 1) * ENC_MAX, :] = one_hot(hits)
    mem_copy.wait()
    expand(0)
    pack(1)

    position = iota((dec_count, 1), 0)
    goal = jnp.full((dec_count, 1), -1, jnp.int32)
    for i in range(PARTNERS):
        within = position - meta[0, i]
        goal = jnp.where((within >= 0) & (within < meta[1, i]), within + i * DEC_MAX, goal)
    unpack_m[...] = one_hot(iota((dec_count, PARTNERS * DEC_MAX), 1) == goal)
    for b in range(enc_count // 256):
        position = iota((256, 1), 0) + b * 256
        goal = jnp.full((256, 1), -1, jnp.int32)
        for slot in range(PARTNERS):
            within = position - meta[2, slot]
            goal = jnp.where(
                (within >= 0) & (within < meta[3, slot]), within + slot * ENC_MAX, goal
            )
        hits = iota((256, PARTNERS * ENC_MAX), 1) == goal
        grad_m[b * 256 : (b + 1) * 256, :] = one_hot(hits)

    expand(1)
    for c in range(2, chunks):
        pack(c)
        expand(c)
    for c in range(chunks):
        attend(c)
        collect(c)
        if c >= 3:
            finish(c - 3)
    for c in range(max(chunks - 3, 0), chunks):
        if c == chunks - 1:
            settle()
        finish(c)

    for c in range(chunks):
        for a in range(2):
            for step in range(1, tensors):
                last_copy(c, a, step).wait()
            last_copy(c, a, 0).wait()


def body(sections, tensors, memory, queries, out_grad, enc_lengths, dec_lengths, readers):
    enc_count, width = memory.shape[1:]
    rows = queries.shape[0]
    dec_count = rows * tensors
    chunks = chunk_count(width)
    piece = width // chunks
    blocks = (chunks, 2, PARTNERS, DEC_MAX, piece)
    peers = max(tensors - 1, 1)
    scalars = (enc_lengths.T, dec_lengths.T, readers.T)
    anywhere = pl.BlockSpec(memory_space=pl.ANY)
    resident = pl.BlockSpec(memory_space=pltpu.VMEM)
    dma = pltpu.SemaphoreType.DMA
    return pl.pallas_call(
        functools.partial(kernel, sections, tensors),
        out_shape=(
            pltpu.VMEM(queries.shape, BF16),
            pltpu.VMEM(queries.shape, BF16),
            pltpu.VMEM(memory.shape, BF16),
        ),
        in_specs=[anywhere] * 6,
        out_specs=(resident,) * 3,
        scratch_shapes=[
            pltpu.VMEM((2, enc_count, width), BF16),
            pltpu.VMEM((chunks, 2, dec_count, piece), BF16),
            pltpu.VMEM(blocks, BF16),
            pltpu.VMEM(blocks, BF16),
            pltpu.VMEM(blocks, BF16),
            pltpu.VMEM(blocks, BF16),
            pltpu.VMEM((chunks, 2, dec_count, piece), BF16),
            pltpu.VMEM((chunks, 2, PARTNERS, ENC_MAX, piece), BF16),
            pltpu.VMEM((2, PARTNERS, ENC_MAX, piece), BF16),
            pltpu.VMEM((2, PARTNERS // 2 * DEC_MAX, dec_count), BF16),
            pltpu.VMEM((dec_count, PARTNERS * DEC_MAX), BF16),
            pltpu.VMEM((PARTNERS // 2, 2 * ENC_MAX, enc_count), BF16),
            pltpu.VMEM((enc_count, PARTNERS * ENC_MAX), BF16),
            *[pltpu.SMEM(array.shape, jnp.int32) for array in scalars],
            pltpu.SMEM((4, PARTNERS), jnp.int32),
            dma((chunks, 2, peers)),
            dma((chunks, 2, peers)),
            dma((chunks, 2)),
            dma((chunks, PARTNERS)),
            dma((chunks, PARTNERS)),
            dma((chunks, PARTNERS)),
            dma((chunks, PARTNERS)),
            dma((chunks, 2, peers)),
            dma((chunks, 2, peers)),
            dma((chunks, 2)),
            dma,
            dma((3,)),
        ],
        compiler_params=pltpu.CompilerParams(
            collective_id=0, has_side_effects=True, vmem_limit_bytes=46 * 1024 * 1024
        ),
    )(memory, queries, out_grad, *scalars)


def solution(mesh):
    placed = (
        P(None, "section", "tensor"),
        P(("section", "tensor"), None),
        P(("section", "tensor"), None),
        P(),
        P(),
        P(),
    )
    return jax.shard_map(
        functools.partial(body, mesh.shape["section"], mesh.shape["tensor"]),
        mesh=mesh,
        in_specs=placed,
        out_specs=(
            P(("section", "tensor"), None),
            P(("section", "tensor"), None),
            P(None, "section", "tensor"),
        ),
        check_vma=False,
    )
```

profile of v0, /device:TPU:0, one launch (start us, length us, event | category | flops | bytes accessed | tf_op | source)
XLA Modules:
  0.0 202.3 jit_solution(8989292422375216619)
XLA Ops:
  0.6 197.0 %shard_map.85 = (bf16[128,4096]{1,0:T(8,128)(2,1)S(1)}, bf16[128,4096]{1,0:T(8,128)(2,1)S(1)}, bf16[2,768,2048]{2,1,0:T(8,128)(2,1)S(1)}) custom-call(bf16[2,768,2048]{2,1,0:T(8,128)(2,1)} %mem_hbm.1, bf16[128,4096]{1,0:T(8,128)(2,1)} %q_hbm.1, bf16[128,4096]{1,0:T(8,128)(2,1)} %g_hbm.1, s32[8,16]{1,0:T(8,128)} %bitcast.3, s32[8,16]{1,0:T(8,128)} %bitcast.4, ...), custom_call_target="tpu_custom_call" | custom-call | tf_op jit(solution)/shard_map/pallas_call | solution.py:368
  197.7 1.0 copy.12
  198.6 1.0 copy.13
  199.6 2.7 %copy.14 = bf16[2,768,2048]{2,1,0:T(8,128)(2,1)} copy(bf16[2,768,2048]{2,1,0:T(8,128)(2,1)S(1)} %get-tuple-element.5) | data formatting | bytes 12582912
where the time goes:
time: 204 us; the launch traced here: 202 us
  Pallas kernels  197 us (97%)
  local copies, waits for them, and re-layouts  4.64 us (2%)
    pallas_call x1, Pallas kernels, body(): pl.pallas_call(functools.partial(kernel, sections, tensors), out_shape=(p...  197 us
    unnamed x3, local copies, waits for them, and re-layouts  4.64 us

commit v1 on v0

--- a/solution.py
+++ b/solution.py
@@ -2,6 +2,7 @@
 
 import jax
 import jax.numpy as jnp
+import numpy as np
 from jax import lax
 from jax.experimental import pallas as pl
 from jax.experimental.pallas import tpu as pltpu
@@ -28,6 +29,20 @@
 
 def chunk_count(width):
     return min(MOST_CHUNKS, width // HD)
+
+
+def staged_kernel(sections, tensors, *refs):
+    inputs, results, staging = refs[:6], refs[6:9], refs[9:12]
+    sem = refs[-1]
+    kernel(sections, tensors, *inputs, *staging, *refs[12:-1])
+    copies = [
+        pltpu.make_async_copy(source, target, sem.at[i])
+        for i, (source, target) in enumerate(zip(staging, results))
+    ]
+    for copy in copies:
+        copy.start()
+    for copy in copies:
+        copy.wait()
 
 
 def kernel(
@@ -353,7 +368,7 @@
             last_copy(c, a, 0).wait()
 
 
-def body(sections, tensors, memory, queries, out_grad, enc_lengths, dec_lengths, readers):
+def padded_body(sections, tensors, staged, memory, queries, out_grad, enc_lengths, dec_lengths, readers):
     enc_count, width = memory.shape[1:]
     rows = queries.shape[0]
     dec_count = rows * tensors
@@ -364,17 +379,18 @@
     scalars = (enc_lengths.T, dec_lengths.T, readers.T)
     anywhere = pl.BlockSpec(memory_space=pl.ANY)
     resident = pl.BlockSpec(memory_space=pltpu.VMEM)
+    results = [array.shape for array in (queries, queries, memory)]
     dma = pltpu.SemaphoreType.DMA
     return pl.pallas_call(
-        functools.partial(kernel, sections, tensors),
-        out_shape=(
-            pltpu.VMEM(queries.shape, BF16),
-            pltpu.VMEM(queries.shape, BF16),
-            pltpu.VMEM(memory.shape, BF16),
+        functools.partial(staged_kernel if staged else kernel, sections, tensors),
+        out_shape=tuple(
+            jax.ShapeDtypeStruct(shape, BF16) if staged else pltpu.VMEM(shape, BF16)
+            for shape in results
         ),
         in_specs=[anywhere] * 6,
-        out_specs=(resident,) * 3,
+        out_specs=(anywhere if staged else resident,) * 3,
         scratch_shapes=[
+            *[pltpu.VMEM(shape, BF16) for shape in results if staged],
             pltpu.VMEM((2, enc_count, width), BF16),
             pltpu.VMEM((chunks, 2, dec_count, piece), BF16),
             pltpu.VMEM(blocks, BF16),
@@ -402,11 +418,778 @@
             dma((chunks, 2)),
             dma,
             dma((3,)),
+            *[dma((3,))] * staged,
         ],
         compiler_params=pltpu.CompilerParams(
-            collective_id=0, has_side_effects=True, vmem_limit_bytes=46 * 1024 * 1024
+            collective_id=0, has_side_effects=True, vmem_limit_bytes=(56 if staged else 46) * 1024 * 1024
         ),
     )(memory, queries, out_grad, *scalars)
+
+
+ZS = 4
+CAP = 640
+RING = 4
+
+
+def packed_kernel(
+    mem_hbm,
+    q_hbm,
+    g_hbm,
+    enc_hbm,
+    dec_hbm,
+    readers_hbm,
+    att_out,
+    qg_out,
+    mg_out,
+    own,
+    inc,
+    out,
+    dsend,
+    drecv,
+    osend,
+    oret,
+    rin,
+    rout,
+    fin_v,
+    mem_v,
+    mg_v,
+    mem_f,
+    d_x,
+    fwd_m,
+    slot_m,
+    ownslot_m,
+    ret_m,
+    fin_m,
+    grad_m,
+    enc_len,
+    dec_len,
+    readers,
+    pre,
+    seg,
+    meta,
+    a_send,
+    a_recv,
+    f_send,
+    f_recv,
+    d_send,
+    d_recv,
+    o_send,
+    o_recv,
+    r_send,
+    r_recv,
+    g_send,
+    g_recv,
+    m_in,
+    m_out,
+    s_in,
+):
+    me = lax.axis_index("section")
+    x = lax.axis_index("tensor")
+    z = lax.div(me, 4)
+    y = lax.rem(lax.div(me, 2), 2)
+    core = lax.rem(me, 2)
+    rows = q_hbm.shape[0]
+    dec_count = 2 * rows
+    enc_count = mem_hbm.shape[1]
+    width = mem_hbm.shape[2]
+    half_width = width // 2
+    chunks = half_width // HD
+    cap = inc.shape[2]
+    scaling = HD ** (-0.5)
+    has_right = z < ZS - 1
+    has_left = z > 0
+    far = jnp.maximum(z, ZS - 1 - z)
+
+    def flip(value, step):
+        return lax.rem(value + step, 2)
+
+    def section_of(zz, yy, cc):
+        return zz * 4 + yy * 2 + cc
+
+    def iota(shape, dim):
+        return lax.broadcasted_iota(jnp.int32, shape, dim)
+
+    def one_hot(hits):
+        return jnp.where(hits, 1.0, 0.0).astype(BF16)
+
+    scalar_copies = [
+        pltpu.make_async_copy(source, target, s_in.at[i])
+        for i, (source, target) in enumerate(
+            ((enc_hbm, enc_len), (dec_hbm, dec_len), (readers_hbm, readers))
+        )
+    ]
+    for copy in scalar_copies:
+        copy.start()
+
+    barrier = pltpu.get_barrier_semaphore()
+
+    def greet(section, tensor):
+        pl.semaphore_signal(
+            barrier,
+            inc=1,
+            device_id={"section": section, "tensor": tensor},
+            device_id_type=MESH,
+        )
+
+    greet(section_of(z, y, core), flip(x, 1))
+    greet(section_of(z, y, flip(core, 1)), flip(x, 1))
+    for e in range(1, 4):
+        greet(section_of(z, flip(y, e // 2), flip(core, e % 2)), x)
+
+    @pl.when(has_right)
+    def _():
+        greet(me + 4, x)
+
+    @pl.when(has_left)
+    def _():
+        greet(me - 4, x)
+
+    pl.semaphore_wait(barrier, 5 + jnp.where(has_right, 1, 0) + jnp.where(has_left, 1, 0))
+
+    def exchange_copy(k, e, a):
+        to_core = flip(core, e // 2)
+        to_x = flip(x, e % 2)
+        source = (q_hbm, g_hbm)[a]
+        column = to_x * width + to_core * half_width + k * HD
+        start = core * dec_count + x * rows
+        args = (
+            source.at[:, pl.ds(pl.multiple_of(column, HD), HD)],
+            own.at[k, pl.ds(pl.multiple_of(start, rows), rows), a * HD : (a + 1) * HD],
+        )
+        if e == 0:
+            return pltpu.make_async_copy(*args, a_recv.at[k, e, a])
+        return pltpu.make_async_remote_copy(
+            src_ref=args[0],
+            dst_ref=args[1],
+            send_sem=a_send.at[k, e, a],
+            recv_sem=a_recv.at[k, e, a],
+            device_id={"section": section_of(z, y, to_core), "tensor": to_x},
+            device_id_type=MESH,
+        )
+
+    def exchange(k):
+        for e in (3, 2, 1, 0):
+            for a in range(2):
+                exchange_copy(k, e, a).start()
+
+    def memory_copy(k, ec):
+        column = flip(core, ec) * half_width + k * HD
+        ring = lax.rem(k, 2)
+        return pltpu.make_async_copy(
+            mem_hbm.at[:, :, pl.ds(pl.multiple_of(column, HD), HD)],
+            mem_v.at[ring, :, :, ec * HD : (ec + 1) * HD],
+            m_in.at[ring, ec],
+        )
+
+    def gradient_copy(k, ec):
+        column = flip(core, ec) * half_width + k * HD
+        ring = lax.rem(k, 2)
+        return pltpu.make_async_copy(
+            mg_v.at[ring, :, :, ec * HD : (ec + 1) * HD],
+            mg_out.at[:, :, pl.ds(pl.multiple_of(column, HD), HD)],
+            m_out.at[ring, ec],
+        )
+
+    def forward_copy(k, d):
+        ring = lax.rem(k, RING)
+        return pltpu.make_async_remote_copy(
+            src_ref=out.at[ring, d],
+            dst_ref=inc.at[k, d],
+            send_sem=f_send.at[ring, d],
+            recv_sem=f_recv.at[k, d],
+            device_id={"section": me + (4, -4)[d]},
+            device_id_type=MESH,
+        )
+
+    def return_copy(k, d):
+        ring = lax.rem(k, RING)
+        return pltpu.make_async_remote_copy(
+            src_ref=rout.at[ring, d],
+            dst_ref=rin.at[k, d],
+            send_sem=r_send.at[ring, d],
+            recv_sem=r_recv.at[k, d],
+            device_id={"section": me + (-4, 4)[d]},
+            device_id_type=MESH,
+        )
+
+    def slot_copy(send, recv, send_sem, recv_sem, k, e):
+        ring = lax.rem(k, RING)
+        if e == 0:
+            return pltpu.make_async_copy(
+                send.at[ring, :, e], recv.at[k, :, e], recv_sem.at[k, e]
+            )
+        return pltpu.make_async_remote_copy(
+            src_ref=send.at[ring, :, e],
+            dst_ref=recv.at[k, :, e],
+            send_sem=send_sem.at[ring, e],
+            recv_sem=recv_sem.at[k, e],
+            device_id={"section": section_of(z, flip(y, e // 2), flip(core, e % 2))},
+            device_id_type=MESH,
+        )
+
+    deliver_copy = functools.partial(slot_copy, dsend, drecv, d_send, d_recv)
+    answer_copy = functools.partial(slot_copy, osend, oret, o_send, o_recv)
+
+    def arrive(copy, e):
+        if e == 0:
+            copy.wait()
+        else:
+            copy.wait_recv()
+
+    def last_copy(k, e, a):
+        to_core = flip(core, e // 2)
+        to_x = flip(x, e % 2)
+        column = x * width + core * half_width + k * HD
+        start = to_core * dec_count + to_x * rows
+        args = (
+            fin_v.at[k, pl.ds(pl.multiple_of(start, rows), rows), a * HD : (a + 1) * HD],
+            (att_out, qg_out)[a].at[:, pl.ds(pl.multiple_of(column, HD), HD)],
+        )
+        if e == 0:
+            return pltpu.make_async_copy(*args, g_recv.at[k, e, a])
+        return pltpu.make_async_remote_copy(
+            src_ref=args[0],
+            dst_ref=args[1],
+            send_sem=g_send.at[k, e, a],
+            recv_sem=g_recv.at[k, e, a],
+            device_id={"section": section_of(z, y, to_core), "tensor": to_x},
+            device_id_type=MESH,
+        )
+
+    def last_arrival(k, e, a):
+        from_core = flip(core, e // 2)
+        from_x = flip(x, e % 2)
+        column = from_x * width + from_core * half_width + k * HD
+        start = core * dec_count + x * rows
+        return pltpu.make_async_remote_copy(
+            src_ref=fin_v.at[
+                k, pl.ds(pl.multiple_of(start, rows), rows), a * HD : (a + 1) * HD
+            ],
+            dst_ref=(att_out, qg_out)[a].at[:, pl.ds(pl.multiple_of(column, HD), HD)],
+            send_sem=g_send.at[k, e, a],
+            recv_sem=g_recv.at[k, e, a],
+            device_id={"section": section_of(z, y, from_core), "tensor": from_x},
+            device_id_type=MESH,
+        )
+
+    for k in range(2):
+        exchange(k)
+    for copy in scalar_copies:
+        copy.wait()
+
+    for n in range(2 * ZS):
+        source = section_of(n // 2, y, n % 2)
+        start = jnp.int32(0)
+        for i in range(PARTNERS):
+            pre[n, i] = start
+            start = start + dec_len[i, source]
+        pre[n, PARTNERS] = start
+
+    OUT_LEN, OUT_AT, OUT_FROM, IN_LEN, IN_AT, IN_FROM = range(6)
+    for d in range(2):
+        out_at, in_at = jnp.int32(0), jnp.int32(0)
+        for n in range(2 * ZS):
+            zs = n // 2
+            if d == 0:
+                begin = pre[n, 2 * z + 2]
+                out_len = jnp.where(zs <= z, dec_count - begin, 0)
+                first = pre[n, 2 * z]
+                in_len = jnp.where(zs < z, dec_count - first, 0)
+            else:
+                begin, first = jnp.int32(0), jnp.int32(0)
+                out_len = jnp.where(zs >= z, pre[n, 2 * z], 0)
+                in_len = jnp.where(zs > z, pre[n, 2 * z + 2], 0)
+            for name, value in (
+                (OUT_LEN, out_len),
+                (OUT_AT, out_at),
+                (OUT_FROM, begin),
+                (IN_LEN, in_len),
+                (IN_AT, in_at),
+                (IN_FROM, first),
+            ):
+                seg[d * 6 + name, n] = value
+            out_at, in_at = out_at + out_len, in_at + in_len
+
+    def part(d, name, n):
+        return seg[d * 6 + name, n]
+
+    def goal_of(count, pieces):
+        position = iota((count, 1), 0)
+        goal = jnp.full((count, 1), -1, jnp.int32)
+        for at, length, column in pieces:
+            within = position - at
+            goal = jnp.where((within >= 0) & (within < length), within + column, goal)
+        return goal
+
+    for d in range(2):
+        pieces = []
+        for n in range(2 * ZS):
+            zs, s = n // 2, n % 2
+            column = jnp.where(
+                zs == z,
+                cap + s * dec_count + part(d, OUT_FROM, n),
+                part(d, IN_AT, n) + part(d, OUT_FROM, n) - part(d, IN_FROM, n),
+            )
+            pieces.append((part(d, OUT_AT, n), part(d, OUT_LEN, n), column))
+        fwd_m[d] = one_hot(iota((cap, cap + 2 * dec_count), 1) == goal_of(cap, pieces))
+
+    @pl.when(~has_left)
+    def _():
+        inc[:, 0] = jnp.zeros(inc.shape[:1] + inc.shape[2:], BF16)
+        rin[:, 1] = jnp.zeros(rin.shape[:1] + rin.shape[2:], BF16)
+
+    @pl.when(~has_right)
+    def _():
+        inc[:, 1] = jnp.zeros(inc.shape[:1] + inc.shape[2:], BF16)
+        rin[:, 0] = jnp.zeros(rin.shape[:1] + rin.shape[2:], BF16)
+
+    def build_slots():
+        for e in range(4):
+            yy, s = flip(y, e // 2), 1 - flip(core, e % 2)
+            i = 2 * z + yy
+            at = slice(e * DEC_MAX, (e + 1) * DEC_MAX)
+            for j in range(ZS - 1):
+                zs = j + jnp.where(j >= z, 1, 0)
+                n = zs * 2 + s
+                d6 = jnp.where(zs < z, 0, 6)
+                column = seg[d6 + IN_AT, n] + pre[n, i] - seg[d6 + IN_FROM, n]
+                within = iota((DEC_MAX, cap), 0)
+                hits = iota((DEC_MAX, cap), 1) - within == column
+                hits = hits & (within < pre[n, i + 1] - pre[n, i])
+                slot_m[j, at] = one_hot(hits)
+            n = z * 2 + s
+            column = s * dec_count + pre[n, i]
+            within = iota((DEC_MAX, 2 * dec_count), 0)
+            hits = iota((DEC_MAX, 2 * dec_count), 1) - within == column
+            hits = hits & (within < pre[n, i + 1] - pre[n, i])
+            ownslot_m[at] = one_hot(hits)
+
+    def build_examples():
+        for t in range(PARTNERS):
+            ey, j = t // ZS, t % ZS
+            zs = z if j == ZS - 1 else j + jnp.where(j >= z, 1, 0)
+            reader = section_of(zs, flip(y, ey), 1 - core)
+            start, begin, size = jnp.int32(0), jnp.int32(0), jnp.int32(0)
+            for i in range(PARTNERS):
+                length = enc_len[i, me]
+                match = readers[i, me] == reader
+                begin = jnp.where(match, start, begin)
+                size = jnp.where(match, length, size)
+                start = start + length
+            meta[0, t] = begin
+            meta[1, t] = size
+        mem_f[:, :, enc_count:] = jnp.zeros((2, 2, ENC_MAX, HD), F32)
+        pieces = [(meta[0, t], meta[1, t], t * ENC_MAX) for t in range(PARTNERS)]
+        goal = goal_of(enc_count, pieces)
+        for b in range(enc_count // 256):
+            at = slice(b * 256, (b + 1) * 256)
+            grad_m[at, :] = one_hot(iota((256, PARTNERS * ENC_MAX), 1) == goal[at])
+
+    remote = (ZS - 1) * 4 * DEC_MAX
+
+    def build_returns():
+        for d in range(2):
+            pieces = []
+            for n in range(2 * ZS):
+                zs, s = n // 2, n % 2
+                valid = part(d, IN_LEN, n) > 0
+                shift = part(d, IN_AT, n) - part(d, IN_FROM, n)
+                j = zs - jnp.where(zs > z, 1, 0)
+                ec = lax.rem(1 - s - core + 2, 2)
+                for yy in range(2):
+                    e = lax.rem(yy - y + 2, 2) * 2 + ec
+                    begin = pre[n, 2 * z + yy]
+                    length = jnp.where(valid, pre[n, 2 * z + yy + 1] - begin, 0)
+                    pieces.append((shift + begin, length, (j * 4 + e) * DEC_MAX))
+                begin = pre[n, 2 * z + 2] if d == 0 else jnp.int32(0)
+                length = dec_count - begin if d == 0 else pre[n, 2 * z]
+                column = remote + part(d, OUT_AT, n)
+                pieces.append((shift + begin, jnp.where(valid, length, 0), column))
+            ret_m[d] = one_hot(iota((cap, remote + cap), 1) == goal_of(cap, pieces))
+
+        pieces = []
+        local = 4 * DEC_MAX
+        for s in range(2):
+            n = z * 2 + s
+            ec = lax.rem(1 - s - core + 2, 2)
+            for yy in range(2):
+                e = lax.rem(yy - y + 2, 2) * 2 + ec
+                begin = pre[n, 2 * z + yy]
+                length = pre[n, 2 * z + yy + 1] - begin
+                pieces.append((s * dec_count + begin, length, e * DEC_MAX))
+            begin = pre[n, 2 * z + 2]
+            at = s * dec_count
+            pieces.append((at + begin, dec_count - begin, local + seg[OUT_AT, n]))
+            pieces.append((at, pre[n, 2 * z], local + cap + seg[6 + OUT_AT, n]))
+        count = 2 * dec_count
+        fin_m[...] = one_hot(iota((count, local + 2 * cap), 1) == goal_of(count, pieces))
+
+    def forward(k, d, starts):
+        ring = lax.rem(k, RING)
+
+        @pl.when(k >= RING)
+        def _():
+            forward_copy(k - RING, d).wait_send()
+
+        @pl.when(jnp.logical_not(starts))
+        def _():
+            forward_copy(k, d).wait_recv()
+            block = matmul(fwd_m[d, :, :cap], inc[k, d], NN)
+            block = block + matmul(fwd_m[d, :, cap:], own[k], NN)
+            out[ring, d] = block.astype(BF16)
+
+        @pl.when(starts)
+        def _():
+            out[ring, d] = matmul(fwd_m[d, :, cap:], own[k], NN).astype(BF16)
+
+        forward_copy(k, d).start()
+
+    def deliver(k):
+        ring = lax.rem(k, RING)
+
+        @pl.when(z == ZS - 1)
+        def _():
+            forward_copy(k, 0).wait_recv()
+
+        @pl.when(z == 0)
+        def _():
+            forward_copy(k, 1).wait_recv()
+
+        @pl.when(k >= RING)
+        def _():
+            for e in range(1, 4):
+                deliver_copy(k - RING, e).wait_send()
+
+        for j in range(ZS - 1):
+            d = jnp.where(j < z, 0, 1)
+            block = matmul(slot_m[j], inc[k, d], NN).astype(BF16)
+            dsend[ring, j] = block.reshape(4, DEC_MAX, 2 * HD)
+        block = matmul(ownslot_m[...], own[k], NN).astype(BF16)
+        dsend[ring, ZS - 1] = block.reshape(4, DEC_MAX, 2 * HD)
+        for e in (3, 2, 1, 0):
+            deliver_copy(k, e).start()
+
+    def attend(k):
+        ring = lax.rem(k, RING)
+        pair = lax.rem(k, 2)
+        for ec in range(2):
+            memory_copy(k, ec).wait()
+        for a in range(2):
+            for ec in range(2):
+                at = slice(ec * HD, (ec + 1) * HD)
+                mem_f[a, ec, :enc_count] = mem_v[pair, a, :, at].astype(F32)
+
+        @pl.when(k + 2 < chunks)
+        def _():
+            for ec in range(2):
+                memory_copy(k + 2, ec).start()
+
+        @pl.when(k >= RING)
+        def _():
+            for e in range(1, 4):
+                answer_copy(k - RING, e).wait_send()
+
+        for e in range(4):
+            arrive(deliver_copy(k, e), e)
+
+        @pl.loop(0, 2)
+        def _(ey):
+            units = [(ey * ZS + j, j, ec) for j in range(ZS) for ec in range(2)]
+            column = iota((DEC_MAX, ENC_MAX), 1)
+
+            def tokens(unit, a):
+                t, j, ec = unit
+                return drecv[k, j, ey * 2 + ec, :, a * HD : (a + 1) * HD]
+
+            def example(unit, a):
+                t, j, ec = unit
+                return mem_f[a, ec, pl.ds(meta[0, t], ENC_MAX)].astype(BF16)
+
+            keys = [example(unit, 0) for unit in units]
+            values = [example(unit, 1) for unit in units]
+            scores = [matmul(tokens(u, 0), key, NT) for u, key in zip(units, keys)]
+            dprobs = [matmul(tokens(u, 1), value, NT) for u, value in zip(units, values)]
+            scores = [jnp.where(column < meta[1, u[0]], s, -jnp.inf) for u, s in zip(units, scores)]
+            most = [jnp.max(s, axis=1, keepdims=True) for s in scores]
+            weights = [jnp.exp((s - m) * scaling) for s, m in zip(scores, most)]
+            scale = [1.0 / jnp.sum(w, axis=1, keepdims=True) for w in weights]
+            probs = [w * r for w, r in zip(weights, scale)]
+            delta = [jnp.sum(w * d, axis=1, keepdims=True) for w, d in zip(probs, dprobs)]
+            low = [w.astype(BF16) for w in probs]
+            dscores = [
+                (w * (d - e)).astype(BF16) for w, d, e in zip(probs, dprobs, delta)
+            ]
+            for i, (t, j, ec) in enumerate(units):
+                e = ey * 2 + ec
+                at = slice(ec * HD, (ec + 1) * HD)
+                osend[ring, j, e, :, :HD] = matmul(low[i], values[i], NN).astype(BF16)
+                block = matmul(dscores[i], keys[i], NN) * scaling
+                osend[ring, j, e, :, HD:] = block.astype(BF16)
+                block = matmul(dscores[i], tokens(units[i], 0), TN) * scaling
+                d_x[0, t, :, at] = block.astype(BF16)
+                d_x[1, t, :, at] = matmul(low[i], tokens(units[i], 1), TN).astype(BF16)
+
+        for e in (3, 2, 1, 0):
+            answer_copy(k, e).start()
+
+    def collect(k):
+        pair = lax.rem(k, 2)
+
+        @pl.when(k >= 2)
+        def _():
+            for ec in range(2):
+                gradient_copy(k - 2, ec).wait()
+
+        for a in range(2):
+
+            @pl.loop(0, enc_count // 256)
+            def _(b):
+                at = pl.ds(pl.multiple_of(b * 256, 256), 256)
+                block = d_x[a].reshape(PARTNERS * ENC_MAX, 2 * HD)
+                mg_v[pair, a, at] = matmul(grad_m[at, :], block, NN).astype(BF16)
+
+        for ec in range(2):
+            gradient_copy(k, ec).start()
+
+    def answers(k):
+        for e in range(4):
+            arrive(answer_copy(k, e), e)
+
+    def give_back(k, d, starts):
+        ring = lax.rem(k, RING)
+
+        @pl.when(k >= RING)
+        def _():
+            return_copy(k - RING, d).wait_send()
+
+        answered = oret[k, : ZS - 1].reshape(remote, 2 * HD)
+
+        @pl.when(jnp.logical_not(starts))
+        def _():
+            return_copy(k, d).wait_recv()
+            block = matmul(ret_m[d, :, :remote], answered, NN)
+            block = block + matmul(ret_m[d, :, remote:], rin[k, d], NN)
+            rout[ring, d] = block.astype(BF16)
+
+        @pl.when(starts)
+        def _():
+            rout[ring, d] = matmul(ret_m[d, :, :remote], answered, NN).astype(BF16)
+
+        return_copy(k, d).start()
+
+    def finish(k):
+        @pl.when(z == 0)
+        def _():
+            return_copy(k, 0).wait_recv()
+
+        @pl.when(z == ZS - 1)
+        def _():
+            return_copy(k, 1).wait_recv()
+
+        local = 4 * DEC_MAX
+        block = matmul(fin_m[:, :local], oret[k, ZS - 1].reshape(local, 2 * HD), NN)
+        for d in range(2):
+            at = local + d * cap
+            block = block + matmul(fin_m[:, at : at + cap], rin[k, d], NN)
+        fin_v[k] = block.astype(BF16)
+        for e in (3, 2, 1, 0):
+            for a in range(2):
+                last_copy(k, e, a).start()
+
+    for k in range(2):
+        for ec in range(2):
+            memory_copy(k, ec).start()
+
+    near = ZS - 1
+    lag = 2
+    back = lag * near + 2
+    settled = lag * far + jnp.where(far < near, 3, 2)
+    steps = chunks + back + lag * near
+
+    def during(k, condition=None):
+        go = (k >= 0) & (k < chunks)
+        if condition is not None:
+            go = go & condition
+        return pl.when(go)
+
+    @pl.loop(0, steps)
+    def _(t):
+        @during(t)
+        def _():
+            for e in range(4):
+                for a in range(2):
+                    arrive(exchange_copy(t, e, a), e)
+
+            @pl.when(t + 2 < chunks)
+            def _():
+                exchange(t + 2)
+
+        @during(t - lag * z, has_right)
+        def _():
+            forward(t - lag * z, 0, z == 0)
+
+        @during(t - lag * (near - z), has_left)
+        def _():
+            forward(t - lag * (near - z), 1, z == near)
+
+        @pl.when(t == 0)
+        def _():
+            build_slots()
+            build_examples()
+            build_returns()
+
+        @during(t - settled)
+        def _():
+            answers(t - settled)
+
+        @during(t - back - lag * (near - z), has_left)
+        def _():
+            give_back(t - back - lag * (near - z), 0, z == near)
+
+        @during(t - back - lag * z, has_right)
+        def _():
+            give_back(t - back - lag * z, 1, z == 0)
+
+        @during(t - lag * far)
+        def _():
+            deliver(t - lag * far)
+
+        @during(t - lag * far - 1)
+        def _():
+            attend(t - lag * far - 1)
+
+        @during(t - lag * far - 1)
+        def _():
+            collect(t - lag * far - 1)
+
+        @during(t - back - lag * far)
+        def _():
+            finish(t - back - lag * far)
+
+    @pl.loop(0, chunks)
+    def _(k):
+        for e in range(4):
+            for a in range(2):
+                if e == 0:
+                    last_copy(k, e, a).wait()
+                else:
+                    exchange_copy(k, e, a).wait_send()
+                    last_copy(k, e, a).wait_send()
+                    last_arrival(k, e, a).wait_recv()
+
+    @pl.loop(chunks - RING, chunks)
+    def _(k):
+        for e in range(1, 4):
+            deliver_copy(k, e).wait_send()
+            answer_copy(k, e).wait_send()
+
+        @pl.when(has_right)
+        def _():
+            forward_copy(k, 0).wait_send()
+            return_copy(k, 1).wait_send()
+
+        @pl.when(has_left)
+        def _():
+            forward_copy(k, 1).wait_send()
+            return_copy(k, 0).wait_send()
+
+    @pl.loop(chunks - 2, chunks)
+    def _(k):
+        for ec in range(2):
+            gradient_copy(k, ec).wait()
+
+
+def packed_body(memory, queries, out_grad, enc_lengths, dec_lengths, readers):
+    enc_count, width = memory.shape[1:]
+    rows = queries.shape[0]
+    count = 4 * rows
+    chunks = width // 2 // HD
+    pair = 2 * HD
+    scalars = (enc_lengths.T, dec_lengths.T, readers.T)
+    anywhere = pl.BlockSpec(memory_space=pl.ANY)
+    dma = pltpu.SemaphoreType.DMA
+    blocks = (ZS, 4, DEC_MAX, pair)
+    local = 4 * DEC_MAX
+    remote = (ZS - 1) * local
+
+    def vmem(*shape):
+        return pltpu.VMEM(shape, BF16)
+
+    return pl.pallas_call(
+        packed_kernel,
+        out_shape=(
+            jax.ShapeDtypeStruct(queries.shape, BF16),
+            jax.ShapeDtypeStruct(queries.shape, BF16),
+            jax.ShapeDtypeStruct(memory.shape, BF16),
+        ),
+        in_specs=[anywhere] * 6,
+        out_specs=(anywhere,) * 3,
+        scratch_shapes=[
+            vmem(chunks, count, pair),
+            vmem(chunks, 2, CAP, pair),
+            vmem(RING, 2, CAP, pair),
+            vmem(RING, *blocks),
+            vmem(chunks, *blocks),
+            vmem(RING, *blocks),
+            vmem(chunks, *blocks),
+            vmem(chunks, 2, CAP, pair),
+            vmem(RING, 2, CAP, pair),
+            vmem(chunks, count, pair),
+            vmem(2, 2, enc_count, pair),
+            vmem(2, 2, enc_count, pair),
+            pltpu.VMEM((2, 2, enc_count + ENC_MAX, HD), F32),
+            vmem(2, PARTNERS, ENC_MAX, pair),
+            vmem(2, CAP, CAP + count),
+            vmem(ZS - 1, local, CAP),
+            vmem(local, count),
+            vmem(2, CAP, remote + CAP),
+            vmem(count, local + 2 * CAP),
+            vmem(enc_count, PARTNERS * ENC_MAX),
+            *[pltpu.SMEM(array.shape, jnp.int32) for array in scalars],
+            pltpu.SMEM((2 * ZS, PARTNERS + 1), jnp.int32),
+            pltpu.SMEM((12, 2 * ZS), jnp.int32),
+            pltpu.SMEM((2, PARTNERS), jnp.int32),
+            dma((chunks, 4, 2)),
+            dma((chunks, 4, 2)),
+            dma((RING, 2)),
+            dma((chunks, 2)),
+            dma((RING, 4)),
+            dma((chunks, 4)),
+            dma((RING, 4)),
+            dma((chunks, 4)),
+            dma((RING, 2)),
+            dma((chunks, 2)),
+            dma((chunks, 4, 2)),
+            dma((chunks, 4, 2)),
+            dma((2, 2)),
+            dma((2, 2)),
+            dma((3,)),
+        ],
+        compiler_params=pltpu.CompilerParams(
+            collective_id=1, has_side_effects=True, vmem_limit_bytes=60 * 1024 * 1024
+        ),
+    )(memory, queries, out_grad, *scalars)
+
+
+def most_rows(dec_lengths):
+    place = np.arange(2 * ZS * 2 * 2 * ZS).reshape(4 * ZS, 2 * ZS)
+    source, half = place // (8 * ZS), place // (4 * ZS) % 2
+    goal = place % (2 * ZS) // 2
+    blocks = []
+    for cut in range(1, ZS):
+        for y in range(2):
+            blocks.append((half == y) & (source < cut) & (goal >= cut))
+            blocks.append((half == y) & (source >= cut) & (goal < cut))
+    counts = jnp.where(np.stack(blocks), dec_lengths, 0)
+    return jnp.max(jnp.sum(counts, axis=(1, 2)))
+
+
+def body(sections, tensors, *args):
+    packs = (sections, tensors) == (4 * ZS, 2)
+    padded = functools.partial(padded_body, sections, tensors, packs)
+    if not packs:
+        return padded(*args)
+    return lax.cond(most_rows(args[4]) <= CAP, packed_body, padded, *args)
 
 
 def solution(mesh):

time: 204 us -> 192 us (0.941)
  Pallas kernels: 197 us -> 180 us
  local copies, waits for them, and re-layouts: 4.64 us -> 8.55 us
    pallas_call x1, Pallas kernels: 197 us -> 180 us  [packed_body(): pl.pallas_call(packed_kernel, out_shape=(jax.ShapeDtypeStruct(queries.sha...]
    unnamed x3, local copies, waits for them, and re-layouts: 4.64 us -> 8.55 us
where the time goes in v1:
time: 192 us
  Pallas kernels  180 us (94%)
  local copies, waits for them, and re-layouts  8.55 us (4%)
    pallas_call x1, Pallas kernels, packed_body(): pl.pallas_call(packed_kernel, out_shape=(jax.ShapeDtypeStruct(queries.sha...  180 us
    unnamed x3, local copies, waits for them, and re-layouts  8.55 us

profile of v1, /device:TPU:0, one launch (start us, length us, event | category | flops | bytes accessed | tf_op | source)
XLA Modules:
  0.0 191.9 jit_solution(14636913544838681361)
XLA Ops:
  0.6 1.0 select_reduce_fusion
  1.6 0.6 reduce_max.9
  2.9 180.4 %conditional.1 = ((bf16[128,4096]{1,0:T(8,128)(2,1)S(1)}, bf16[128,4096]{1,0:T(8,128)(2,1)S(1)}, bf16[2,768,2048]{2,1,0:T(8,128)(2,1)})) conditional(s32[]{:T(128)} %convert_element_type.3, (s32[16,8]{0,1:T(8,128)}, s32[16,8]{0,1:T(8,128)}, s32[16,8]{0,1:T(8,128)}, bf16[2,768,2048]{2,1,0:T(8,128)(2,1)}, bf16[128,4096]{1,0:T(8,128)(2,1)}, ...), branch_computations={%region_2.3_spmd, %region_3.4_spmd} | conditional | bytes 8 | solution.py:1192
  3.1 180.0 %branch_1_fun.1 = (bf16[128,4096]{1,0:T(8,128)(2,1)S(1)}, bf16[128,4096]{1,0:T(8,128)(2,1)S(1)}, bf16[2,768,2048]{2,1,0:T(8,128)(2,1)}) custom-call(bf16[2,768,2048]{2,1,0:T(8,128)(2,1)} %get-tuple-element.30.mem_hbm, bf16[128,4096]{1,0:T(8,128)(2,1)} %get-tuple-element.31.q_hbm, bf16[128,4096]{1,0:T(8,128)(2,1)} %get-tuple-element.32.g_hbm, ...), custom_call_target="tpu_custom_call" | custom-call | tf_op jit(solution)/shard_map/cond/branch_1_fun/pallas_call | solution.py:1118
  183.4 1.0 copy.26
  184.3 1.0 copy.27
  185.3 6.6 %copy.28 = bf16[2,768,2048]{2,1,0:T(8,128)(2,1)} copy(bf16[2,768,2048]{2,1,0:T(8,128)(2,1)} %get-tuple-element.59) | data formatting | bytes 12582912

commit v2 on v1

--- a/solution.py
+++ b/solution.py
@@ -1001,7 +1001,7 @@
             memory_copy(k, ec).start()
 
     near = ZS - 1
-    lag = 2
+    lag = 1
     back = lag * near + 2
     settled = lag * far + jnp.where(far < near, 3, 2)
     steps = chunks + back + lag * near
@@ -1038,6 +1038,10 @@
             build_examples()
             build_returns()
 
+        @during(t - lag * far)
+        def _():
+            deliver(t - lag * far)
+
         @during(t - settled)
         def _():
             answers(t - settled)
@@ -1049,10 +1053,6 @@
         @during(t - back - lag * z, has_right)
         def _():
             give_back(t - back - lag * z, 1, z == 0)
-
-        @during(t - lag * far)
-        def _():
-            deliver(t - lag * far)
 
         @during(t - lag * far - 1)
         def _():

time: 192 us -> 171 us (0.89)
  Pallas kernels: 180 us -> 158 us
    pallas_call x1, Pallas kernels: 180 us -> 158 us  [packed_body(): pl.pallas_call(packed_kernel, out_shape=(jax.ShapeDtypeStruct(queries.sha...]
where the time goes in v2:
time: 171 us; the launch traced here: 170 us
  Pallas kernels  158 us (92%)
  local copies, waits for them, and re-layouts  8.55 us (5%)
    pallas_call x1, Pallas kernels, packed_body(): pl.pallas_call(packed_kernel, out_shape=(jax.ShapeDtypeStruct(queries.sha...  158 us
    unnamed x3, local copies, waits for them, and re-layouts  8.55 us

profile of v2, /device:TPU:0, one launch (start us, length us, event | category | flops | bytes accessed | tf_op | source)
XLA Modules:
  0.0 170.4 jit_solution(17655651220566207593)
XLA Ops:
  0.6 1.0 select_reduce_fusion
  1.6 0.6 reduce_max.9
  2.9 158.9 %conditional.1 = ((bf16[128,4096]{1,0:T(8,128)(2,1)S(1)}, bf16[128,4096]{1,0:T(8,128)(2,1)S(1)}, bf16[2,768,2048]{2,1,0:T(8,128)(2,1)})) conditional(s32[]{:T(128)} %convert_element_type.3, (s32[16,8]{0,1:T(8,128)}, s32[16,8]{0,1:T(8,128)}, s32[16,8]{0,1:T(8,128)}, bf16[2,768,2048]{2,1,0:T(8,128)(2,1)}, bf16[128,4096]{1,0:T(8,128)(2,1)}, ...), branch_computations={%region_2.3_spmd, %region_3.4_spmd} | conditional | bytes 8 | solution.py:1192
  3.1 158.5 %branch_1_fun.1 = (bf16[128,4096]{1,0:T(8,128)(2,1)S(1)}, bf16[128,4096]{1,0:T(8,128)(2,1)S(1)}, bf16[2,768,2048]{2,1,0:T(8,128)(2,1)}) custom-call(bf16[2,768,2048]{2,1,0:T(8,128)(2,1)} %get-tuple-element.30.mem_hbm, bf16[128,4096]{1,0:T(8,128)(2,1)} %get-tuple-element.31.q_hbm, bf16[128,4096]{1,0:T(8,128)(2,1)} %get-tuple-element.32.g_hbm, ...), custom_call_target="tpu_custom_call" | custom-call | tf_op jit(solution)/shard_map/cond/branch_1_fun/pallas_call | solution.py:1118
  161.9 1.0 copy.26
  162.9 1.0 copy.27
  163.8 6.6 %copy.28 = bf16[2,768,2048]{2,1,0:T(8,128)(2,1)} copy(bf16[2,768,2048]{2,1,0:T(8,128)(2,1)} %get-tuple-element.59) | data formatting | bytes 12582912

commit v3 on v2

--- a/solution.py
+++ b/solution.py
@@ -428,6 +428,32 @@
 
 ZS = 4
 CAP = 640
+OUTER = 544
+
+
+class Hop:
+    def __init__(self, make, middle):
+        self.make, self.middle = make, middle
+
+    def each(self, action):
+        @pl.when(self.middle)
+        def _():
+            action(self.make(CAP))
+
+        @pl.when(jnp.logical_not(self.middle))
+        def _():
+            action(self.make(OUTER))
+
+    def start(self):
+        self.each(lambda copy: copy.start())
+
+    def wait_send(self):
+        self.each(lambda copy: copy.wait_send())
+
+    def wait_recv(self):
+        self.each(lambda copy: copy.wait_recv())
+
+
 RING = 4
 
 
@@ -590,27 +616,35 @@
             m_out.at[ring, ec],
         )
 
-    def forward_copy(k, d):
+    def forward_copy(k, d, arrives=False):
         ring = lax.rem(k, RING)
-        return pltpu.make_async_remote_copy(
-            src_ref=out.at[ring, d],
-            dst_ref=inc.at[k, d],
-            send_sem=f_send.at[ring, d],
-            recv_sem=f_recv.at[k, d],
-            device_id={"section": me + (4, -4)[d]},
-            device_id_type=MESH,
-        )
-
-    def return_copy(k, d):
+
+        def make(count):
+            return pltpu.make_async_remote_copy(
+                src_ref=out.at[ring, d, :count],
+                dst_ref=inc.at[k, d, :count],
+                send_sem=f_send.at[ring, d],
+                recv_sem=f_recv.at[k, d],
+                device_id={"section": me + (4, -4)[d]},
+                device_id_type=MESH,
+            )
+
+        return Hop(make, (z == 1, z == 2)[d ^ arrives])
+
+    def return_copy(k, d, arrives=False):
         ring = lax.rem(k, RING)
-        return pltpu.make_async_remote_copy(
-            src_ref=rout.at[ring, d],
-            dst_ref=rin.at[k, d],
-            send_sem=r_send.at[ring, d],
-            recv_sem=r_recv.at[k, d],
-            device_id={"section": me + (-4, 4)[d]},
-            device_id_type=MESH,
-        )
+
+        def make(count):
+            return pltpu.make_async_remote_copy(
+                src_ref=rout.at[ring, d, :count],
+                dst_ref=rin.at[k, d, :count],
+                send_sem=r_send.at[ring, d],
+                recv_sem=r_recv.at[k, d],
+                device_id={"section": me + (-4, 4)[d]},
+                device_id_type=MESH,
+            )
+
+        return Hop(make, (z == 2, z == 1)[d ^ arrives])
 
     def slot_copy(send, recv, send_sem, recv_sem, k, e):
         ring = lax.rem(k, RING)
@@ -731,7 +765,22 @@
                 part(d, IN_AT, n) + part(d, OUT_FROM, n) - part(d, IN_FROM, n),
             )
             pieces.append((part(d, OUT_AT, n), part(d, OUT_LEN, n), column))
-        fwd_m[d] = one_hot(iota((cap, cap + 2 * dec_count), 1) == goal_of(cap, pieces))
+
+        @pl.when((has_right, has_left)[d])
+        def _():
+            hits = iota((cap, cap + 2 * dec_count), 1) == goal_of(cap, pieces)
+            fwd_m[d] = one_hot(hits)
+
+    for d in range(2):
+        tail = jnp.zeros((chunks, cap - OUTER, 2 * HD), BF16)
+
+        @pl.when(z != (2, 1)[d])
+        def _():
+            inc[:, d, OUTER:] = tail
+
+        @pl.when(z != (1, 2)[d])
+        def _():
+            rin[:, d, OUTER:] = tail
 
     @pl.when(~has_left)
     def _():
@@ -805,7 +854,11 @@
                 length = dec_count - begin if d == 0 else pre[n, 2 * z]
                 column = remote + part(d, OUT_AT, n)
                 pieces.append((shift + begin, jnp.where(valid, length, 0), column))
-            ret_m[d] = one_hot(iota((cap, remote + cap), 1) == goal_of(cap, pieces))
+
+            @pl.when((has_left, has_right)[d])
+            def _():
+                hits = iota((cap, remote + cap), 1) == goal_of(cap, pieces)
+                ret_m[d] = one_hot(hits)
 
         pieces = []
         local = 4 * DEC_MAX
@@ -833,7 +886,7 @@
 
         @pl.when(jnp.logical_not(starts))
         def _():
-            forward_copy(k, d).wait_recv()
+            forward_copy(k, d, True).wait_recv()
             block = matmul(fwd_m[d, :, :cap], inc[k, d], NN)
             block = block + matmul(fwd_m[d, :, cap:], own[k], NN)
             out[ring, d] = block.astype(BF16)
@@ -849,11 +902,11 @@
 
         @pl.when(z == ZS - 1)
         def _():
-            forward_copy(k, 0).wait_recv()
+            forward_copy(k, 0, True).wait_recv()
 
         @pl.when(z == 0)
         def _():
-            forward_copy(k, 1).wait_recv()
+            forward_copy(k, 1, True).wait_recv()
 
         @pl.when(k >= RING)
         def _():
@@ -966,7 +1019,7 @@
 
         @pl.when(jnp.logical_not(starts))
         def _():
-            return_copy(k, d).wait_recv()
+            return_copy(k, d, True).wait_recv()
             block = matmul(ret_m[d, :, :remote], answered, NN)
             block = block + matmul(ret_m[d, :, remote:], rin[k, d], NN)
             rout[ring, d] = block.astype(BF16)
@@ -980,11 +1033,11 @@
     def finish(k):
         @pl.when(z == 0)
         def _():
-            return_copy(k, 0).wait_recv()
+            return_copy(k, 0, True).wait_recv()
 
         @pl.when(z == ZS - 1)
         def _():
-            return_copy(k, 1).wait_recv()
+            return_copy(k, 1, True).wait_recv()
 
         local = 4 * DEC_MAX
         block = matmul(fin_m[:, :local], oret[k, ZS - 1].reshape(local, 2 * HD), NN)
@@ -1171,17 +1224,19 @@
     )(memory, queries, out_grad, *scalars)
 
 
-def most_rows(dec_lengths):
+def fits(dec_lengths):
     place = np.arange(2 * ZS * 2 * 2 * ZS).reshape(4 * ZS, 2 * ZS)
     source, half = place // (8 * ZS), place // (4 * ZS) % 2
     goal = place % (2 * ZS) // 2
     blocks = []
+    cuts = np.repeat(np.arange(1, ZS), 4)
     for cut in range(1, ZS):
         for y in range(2):
             blocks.append((half == y) & (source < cut) & (goal >= cut))
             blocks.append((half == y) & (source >= cut) & (goal < cut))
     counts = jnp.where(np.stack(blocks), dec_lengths, 0)
-    return jnp.max(jnp.sum(counts, axis=(1, 2)))
+    most = np.array([CAP if cut == ZS // 2 else OUTER for cut in cuts])
+    return jnp.all(jnp.sum(counts, axis=(1, 2)) <= most)
 
 
 def body(sections, tensors, *args):
@@ -1189,7 +1244,7 @@
     padded = functools.partial(padded_body, sections, tensors, packs)
     if not packs:
         return padded(*args)
-    return lax.cond(most_rows(args[4]) <= CAP, packed_body, padded, *args)
+    return lax.cond(fits(args[4]), packed_body, padded, *args)
 
 
 def solution(mesh):

time: 171 us -> 169 us (0.988)
  Pallas kernels: 158 us -> 155 us
    pallas_call x1, Pallas kernels: 158 us -> 155 us  [packed_body(): pl.pallas_call(packed_kernel, out_shape=(jax.ShapeDtypeStruct(queries.sha...]
where the time goes in v3:
time: 169 us; the launch traced here: 168 us
  Pallas kernels  155 us (92%)
  local copies, waits for them, and re-layouts  8.55 us (5%)
  other arithmetic  2.32 us (1%)
    pallas_call x1, Pallas kernels, packed_body(): pl.pallas_call(packed_kernel, out_shape=(jax.ShapeDtypeStruct(queries.sha...  155 us
    unnamed x3, local copies, waits for them, and re-layouts  8.55 us

profile of v3, /device:TPU:0, one launch (start us, length us, event | category | flops | bytes accessed | tf_op | source)
XLA Modules:
  0.0 167.9 jit_solution(7033197970412538480)
XLA Ops:
  0.6 1.0 select_reduce_fusion
  1.6 1.3 compare_reduce_fusion
  3.6 155.7 %conditional.1 = ((bf16[128,4096]{1,0:T(8,128)(2,1)S(1)}, bf16[128,4096]{1,0:T(8,128)(2,1)S(1)}, bf16[2,768,2048]{2,1,0:T(8,128)(2,1)})) conditional(s32[]{:T(128)} %convert_element_type.3, (s32[16,8]{0,1:T(8,128)}, s32[16,8]{0,1:T(8,128)}, s32[16,8]{0,1:T(8,128)}, bf16[2,768,2048]{2,1,0:T(8,128)(2,1)}, bf16[128,4096]{1,0:T(8,128)(2,1)}, ...), branch_computations={%region_2.3_spmd, %region_3.4_spmd} | conditional | bytes 8 | solution.py:1247
  3.8 155.3 %branch_1_fun.1 = (bf16[128,4096]{1,0:T(8,128)(2,1)S(1)}, bf16[128,4096]{1,0:T(8,128)(2,1)S(1)}, bf16[2,768,2048]{2,1,0:T(8,128)(2,1)}) custom-call(bf16[2,768,2048]{2,1,0:T(8,128)(2,1)} %get-tuple-element.30.mem_hbm, bf16[128,4096]{1,0:T(8,128)(2,1)} %get-tuple-element.31.q_hbm, bf16[128,4096]{1,0:T(8,128)(2,1)} %get-tuple-element.32.g_hbm, ...), custom_call_target="tpu_custom_call" | custom-call | tf_op jit(solution)/shard_map/cond/branch_1_fun/pallas_call | solution.py:1171
  159.3 1.0 copy.27
  160.3 1.0 copy.28
  161.3 6.6 %copy.29 = bf16[2,768,2048]{2,1,0:T(8,128)(2,1)} copy(bf16[2,768,2048]{2,1,0:T(8,128)(2,1)} %get-tuple-element.59) | data formatting | bytes 12582912

commit v4 on v3

--- a/solution.py
+++ b/solution.py
@@ -994,12 +994,8 @@
                 gradient_copy(k - 2, ec).wait()
 
         for a in range(2):
-
-            @pl.loop(0, enc_count // 256)
-            def _(b):
-                at = pl.ds(pl.multiple_of(b * 256, 256), 256)
-                block = d_x[a].reshape(PARTNERS * ENC_MAX, 2 * HD)
-                mg_v[pair, a, at] = matmul(grad_m[at, :], block, NN).astype(BF16)
+            block = d_x[a].reshape(PARTNERS * ENC_MAX, 2 * HD)
+            mg_v[pair, a] = matmul(grad_m[...], block, NN).astype(BF16)
 
         for ec in range(2):
             gradient_copy(k, ec).start()

time: 169 us -> 167 us (0.988)
  no operation moved by 1% of the time
where the time goes in v4:
time: 167 us
  Pallas kernels  154 us (92%)
  local copies, waits for them, and re-layouts  8.55 us (5%)
  other arithmetic  2.32 us (1%)
    pallas_call x1, Pallas kernels, packed_body(): pl.pallas_call(packed_kernel, out_shape=(jax.ShapeDtypeStruct(queries.sha...  154 us
    unnamed x3, local copies, waits for them, and re-layouts  8.55 us

profile of v4, /device:TPU:0, one launch (start us, length us, event | category | flops | bytes accessed | tf_op | source)
XLA Modules:
  0.0 167.0 jit_solution(15116415312909896315)
XLA Ops:
  0.6 1.0 select_reduce_fusion
  1.6 1.3 compare_reduce_fusion
  3.6 154.8 %conditional.1 = ((bf16[128,4096]{1,0:T(8,128)(2,1)S(1)}, bf16[128,4096]{1,0:T(8,128)(2,1)S(1)}, bf16[2,768,2048]{2,1,0:T(8,128)(2,1)})) conditional(s32[]{:T(128)} %convert_element_type.3, (s32[16,8]{0,1:T(8,128)}, s32[16,8]{0,1:T(8,128)}, s32[16,8]{0,1:T(8,128)}, bf16[2,768,2048]{2,1,0:T(8,128)(2,1)}, bf16[128,4096]{1,0:T(8,128)(2,1)}, ...), branch_computations={%region_2.3_spmd, %region_3.4_spmd} | conditional | bytes 8 | solution.py:1243
  3.8 154.4 %branch_1_fun.1 = (bf16[128,4096]{1,0:T(8,128)(2,1)S(1)}, bf16[128,4096]{1,0:T(8,128)(2,1)S(1)}, bf16[2,768,2048]{2,1,0:T(8,128)(2,1)}) custom-call(bf16[2,768,2048]{2,1,0:T(8,128)(2,1)} %get-tuple-element.30.mem_hbm, bf16[128,4096]{1,0:T(8,128)(2,1)} %get-tuple-element.31.q_hbm, bf16[128,4096]{1,0:T(8,128)(2,1)} %get-tuple-element.32.g_hbm, ...), custom_call_target="tpu_custom_call" | custom-call | tf_op jit(solution)/shard_map/cond/branch_1_fun/pallas_call | solution.py:1167
  158.4 1.0 copy.27
  159.4 1.0 copy.28
  160.4 6.6 %copy.29 = bf16[2,768,2048]{2,1,0:T(8,128)(2,1)} copy(bf16[2,768,2048]{2,1,0:T(8,128)(2,1)} %get-tuple-element.59) | data formatting | bytes 12582912
